TPU v7x, 512 devices: a whole 4x4x16 slice. The times are simulated.
512 devices in a mesh: dp: 64 (over y, x, z_lo), tensor: 8 (over z_hi, core).
Axes of the slice: x: 4, y: 4, z: 16 (z_hi: 4, z_lo: 4; z = z_hi * 4 + z_lo), core: 2. Of those that a mesh axis runs over, the one named last changes fastest.
Arguments:
- grad_out: bfloat16 [16384, 4096], P('dp'), may hold values from -4 to 4
- hidden: bfloat16 [16384, 11008], P('dp', 'tensor'), may hold values from -6 to 6
- proj_basis: bfloat16 [4096, 512], P('dp'), may hold values from -0.09375 to 0.09375
- weight: bfloat16 [4096, 11008], P('dp', 'tensor'), may hold values from -0.75 to 0.75
- first_moment: float32 [512, 11008], P('dp', 'tensor'), may hold values from -6 to 6
- second_moment: float32 [512, 11008], P('dp', 'tensor'), may hold values from 0.5 to 4
Outputs:
- new_weight: bfloat16 [4096, 11008], P('dp')
- new_first: float32 [512, 11008], P('dp', 'tensor')
- new_second: float32 [512, 11008], P('dp', 'tensor')
All inputs are finite; a program needn't handle non-finite values.
Results may differ from a plain program's by a relative error of at most 0.0053.
Values may be sent and summed in bfloat16 or wider, within the bound.
A program may use at most 64 MiB of HBM per device.

v0:
```python
import jax
import jax.numpy as jnp
from jax import lax
from jax.sharding import PartitionSpec as P


def local(grad_out, hidden, proj_basis, weight, first_moment, second_moment):
    columns = grad_out
    projected = jnp.dot(
        columns,
        lax.all_gather(proj_basis, "dp", axis=0, tiled=True),
        preferred_element_type=jnp.float32,
    ).astype(jnp.bfloat16)
    grad_low = lax.psum_scatter(
        lax.dot_general(
            projected, hidden, (((0,), (0,)), ((), ())), preferred_element_type=jnp.float32
        ),
        "dp",
        scatter_dimension=0,
        tiled=True,
    )
    new_first = 0.9 * first_moment + 0.1 * grad_low
    new_second = 0.999 * second_moment + 0.001 * grad_low * grad_low
    direction = (new_first / (jnp.sqrt(new_second) + 1e-08)).astype(jnp.bfloat16)
    columns = proj_basis
    update = jnp.dot(
        columns,
        lax.all_gather(direction, "dp", axis=0, tiled=True),
        preferred_element_type=jnp.float32,
    )
    new_local = (weight.astype(jnp.float32) - 0.1 * update).astype(jnp.bfloat16)
    new_weight = lax.all_gather(new_local, "tensor", axis=1, tiled=True)
    return (new_weight, new_first, new_second)


def solution(mesh):
    return jax.shard_map(
        local,
        mesh=mesh,
        in_specs=(
            P("dp", None),
            P("dp", "tensor"),
            P("dp", None),
            P("dp", "tensor"),
            P("dp", "tensor"),
            P("dp", "tensor"),
        ),
        out_specs=(P("dp", None), P("dp", "tensor"), P("dp", "tensor")),
        check_vma=False,
    )
```

profile of v0, /device:TPU:1, one launch (start us, length us, event | category | flops | bytes accessed | tf_op | source)
XLA Modules:
  0.0 1529.4 jit_solution(15125099179890619975)
XLA Ops:
  7.2 0.0 copy-start
  7.2 0.0 all-gather.5.cloned.1.call-start
  7.2 0.7 all-gather.5.cloned.1.call-update
  7.9 0.0 all-reduce.3.cloned.1.call-start
  8.0 330.0 %all-gather.5.cloned.1.call-done = bf16[4096,512]{1,0:T(8,128)(2,1)} async-done(((bf16[64,512]{1,0:T(8,128)(2,1)}), bf16[4096,512]{1,0:T(8,128)(2,1)}) %all-gather.5.cloned.1.call-update) | async-done | bytes 4194320 | tf_op jit(solution)/shard_map/all_gather | solution.py:11
  337.9 0.0 copy-done
  337.9 5.8 fusion.4
  343.7 0.0 all-reduce.3.cloned.1.call-update
  343.8 0.0 all-gather.7.cloned.1.call-start
  343.8 1.3 dynamic-slice
  345.8 725.4 %all-reduce.3.cloned.1.call-done = f32[512,1376]{1,0:T(8,128)} async-done(((f32[512,1376]{1,0:T(8,128)}), f32[512,1376]{1,0:T(8,128)}) %all-reduce.3.cloned.1.call-update) | async-done | bytes 2818064
  1071.2 0.0 copy-done.3
  1071.2 0.0 copy-done.4
  1071.2 1.4 divide_convert_fusion
  1072.7 0.0 all-gather.7.cloned.1.call-update
  1072.7 0.0 all-gather.9.cloned.1.call-start
  1072.7 346.7 %all-gather.7.cloned.1.call-done = bf16[512,1376]{1,0:T(8,128)(2,1)} async-done(((bf16[8,1376]{1,0:T(8,128)(2,1)}), bf16[512,1376]{1,0:T(8,128)(2,1)}) %all-gather.7.cloned.1.call-update) | async-done | bytes 1409040 | tf_op jit(solution)/shard_map/all_gather | solution.py:28
  1419.4 0.0 copy-done.1
  1419.4 0.0 copy-done.2
  1419.4 2.4 fusion.3
  1421.8 0.0 all-gather.9.cloned.1.call-update
  1421.9 96.7 %all-gather.9.cloned.1.call-done = bf16[8,1376,64]{1,2,0:T(8,128)(2,1)} async-done(((bf16[1,1376,64]{1,2,0:T(8,128)(2,1)}), bf16[8,1376,64]{1,2,0:T(8,128)(2,1)}) %all-gather.9.cloned.1.call-update) | async-done | bytes 1409040 | tf_op jit(solution)/shard_map/all_gather | solution.py:32
  1518.6 2.2 copy.10
  1520.8 2.1 reshape.7
  (4 shorter events, 0.0 us)
Async XLA Ops:
  7.2 330.8 %copy-start = (bf16[256,4096]{1,0:T(8,128)(2,1)S(1)}, bf16[256,4096]{1,0:T(8,128)(2,1)}, u32[]{:S(2)}) copy-start(bf16[256,4096]{1,0:T(8,128)(2,1)} %param.6) | copy-start | bytes 6291460
  7.2 330.7 %all-gather.5.cloned.1.call-start = ((), (), s32[]{:S(2)}) async-start(), calls=%async_computation | async-start | bytes 4259840 | tf_op jit(solution)/shard_map/all_gather | solution.py:11
  7.9 1063.3 %all-reduce.3.cloned.1.call-start = ((), (), s32[]{:S(2)}) async-start(), calls=%async_computation.3 | async-start | bytes 5767168
  343.7 727.5 %copy-start.3 = (f32[8,1376]{1,0:T(8,128)S(1)}, f32[8,1376]{1,0:T(8,128)}, u32[]{:S(2)}) copy-start(f32[8,1376]{1,0:T(8,128)} %param.11) | copy-start | bytes 132100
  343.7 727.5 %copy-start.4 = (f32[8,1376]{1,0:T(8,128)S(1)}, f32[8,1376]{1,0:T(8,128)}, u32[]{:S(2)}) copy-start(f32[8,1376]{1,0:T(8,128)} %param.10) | copy-start | bytes 132100
  343.7 1075.7 %copy-start.1 = (bf16[64,512]{1,0:T(8,128)(2,1)S(1)}, bf16[64,512]{1,0:T(8,128)(2,1)}, u32[]{:S(2)}) copy-start(bf16[64,512]{1,0:T(8,128)(2,1)} %param.8) | copy-start | bytes 196612
  343.7 1075.7 %copy-start.2 = (bf16[64,1376]{1,0:T(8,128)(2,1)S(1)}, bf16[64,1376]{1,0:T(8,128)(2,1)}, u32[]{:S(2)}) copy-start(bf16[64,1376]{1,0:T(8,128)(2,1)} %param.9) | copy-start | bytes 528388
  343.8 1075.6 %all-gather.7.cloned.1.call-start = ((), (), s32[]{:S(2)}) async-start(), calls=%async_computation.1 | async-start | bytes 1464320 | tf_op jit(solution)/shard_map/all_gather | solution.py:28
  1072.7 445.9 %all-gather.9.cloned.1.call-start = ((), (), s32[]{:S(2)}) async-start(), calls=%async_computation.2 | async-start | bytes 1622016 | tf_op jit(solution)/shard_map/all_gather | solution.py:32
Sparse Core Ops, SparseCore 0:
  10.1 327.7 all-gather.4
  343.9 727.2 all-reduce.2
  1074.1 345.2 all-gather.6
  1422.2 96.3 all-gather.8
where the time goes:
time: 1530 us
  waiting for transfers between devices  1500 us (98%)
    unnamed x5, waiting for transfers between devices  726 us
    all_gather x1, waiting for transfers between devices, local(): lax.all_gather(direction, 'dp', axis=0, tiled=True)  347 us
    all_gather x1, waiting for transfers between devices, local(): lax.all_gather(proj_basis, 'dp', axis=0, tiled=True)  330 us
    all_gather x1, waiting for transfers between devices, local(): new_weight = lax.all_gather(new_local, 'tensor', axis=1, tiled=True)  96.7 us
  transfers between devices with their start and end apart: 4, of which 4 were waited for; matrix products, arithmetic and copies ran while one was open for 0% of the time, Pallas kernels for 0%

commit v1 on v0

v1 whole, which is shorter than its diff:
```python
import functools

import jax
import jax.numpy as jnp
from jax import lax
from jax.experimental import pallas as pl
from jax.experimental.pallas import tpu as pltpu
from jax.sharding import PartitionSpec as P

MESH = pl.DeviceIdType.MESH
F32 = jnp.float32
BF16 = jnp.bfloat16

WIDTH = 1376
CHUNKS = ((0, 512, 512), (512, 512, 512), (1024, 352, 384))
HALF = 256
SLOT = 1408


def pack(rows):
    low, high = rows[:, :HALF], rows[:, HALF:]
    if high.shape[1] < HALF:
        high = jnp.concatenate(
            [high, jnp.zeros((8, HALF - high.shape[1]), high.dtype)], axis=1
        )
    return jnp.concatenate([low, high], axis=0)


def unpack(block):
    return jnp.concatenate([block[:8], block[8:]], axis=1)


def kernel(
    grad_ref, hidden_ref, basis_ref, weight_ref, first_ref, second_ref,
    slots_ref, new_first_ref, new_second_ref,
    grad, hidden, basis, weight, first, second, load_sem,
    gathered, expand, proj, dirs,
    part0, part1, part2, ra0, ra1, ra2, sa0, sa1, sa2, rb0, rb1, rb2,
    sz, szf, rz, steps, local_new, own_sem,
    a_send, a_recv, p_send, p_recv, c_send, c_recv,
):
    parts, ras, sas, rbs = (part0, part1, part2), (ra0, ra1, ra2), (sa0, sa1, sa2), (rb0, rb1, rb2)
    dp, tensor = lax.axis_index("dp"), lax.axis_index("tensor")
    y, x, z = dp // 16, (dp // 4) % 4, dp % 4
    hi, core = tensor // 2, tensor % 2
    even = core == 0
    a, b = jnp.where(even, y, x), jnp.where(even, x, y)

    def device(a_, b_, z_, hi_, core_):
        y_, x_ = jnp.where(even, a_, b_), jnp.where(even, b_, a_)
        return ((y_ * 4 + x_) * 4 + z_, hi_ * 2 + core_)

    a_peers = [device((a + k) % 4, b, z, hi, core) for k in (1, 2, 3)]
    b_peers = [device(a, (b + k) % 4, z, hi, core) for k in (1, 2, 3)]
    z_peers = [device(a, b, (z + k) % 4, hi, core) for k in (1, 2, 3)]
    hi_next = device(a, b, z, (hi + 1) % 4, core)
    hi_prev = device(a, b, z, (hi + 3) % 4, core)
    sibling = (dp, hi * 2 + 1 - core)

    loads = [
        pltpu.make_async_copy(basis_ref, basis, load_sem.at[0]),
        pltpu.make_async_copy(grad_ref, grad, load_sem.at[1]),
        pltpu.make_async_copy(hidden_ref, hidden.at[pl.ds(0, WIDTH)], load_sem.at[2]),
        pltpu.make_async_copy(first_ref, first, load_sem.at[3]),
        pltpu.make_async_copy(second_ref, second, load_sem.at[4]),
        pltpu.make_async_copy(weight_ref, weight, load_sem.at[5]),
    ]
    for load in loads:
        load.start()

    barrier = pltpu.get_barrier_semaphore()
    friends = a_peers + b_peers + z_peers + [hi_next, hi_prev, sibling]
    for friend in friends:
        pl.semaphore_signal(barrier, inc=1, device_id=friend, device_id_type=MESH)

    sends = []

    def send(src, dst, send_sem, recv_sem, to):
        copy = pltpu.make_async_remote_copy(
            src_ref=src, dst_ref=dst, send_sem=send_sem, recv_sem=recv_sem,
            device_id=to, device_id_type=MESH,
        )
        copy.start()
        sends.append(copy)
        return copy

    hidden[pl.ds(WIDTH, SLOT - WIDTH)] = jnp.zeros((SLOT - WIDTH, 256), BF16)
    dirs[...] = jnp.zeros_like(dirs)
    loads[0].wait()
    mine = a * 16 + b * 4 + z
    columns = pl.ds(pl.multiple_of(core * 256, 256), 256)
    gathered[mine] = basis[:, columns]
    pl.semaphore_wait(barrier, len(friends))

    wait_z = [send(gathered.at[mine], gathered.at[mine], a_send.at[k], a_recv.at[k], z_peers[k]) for k in range(3)]

    lane = lax.broadcasted_iota(jnp.int32, (512, 1024), 1)
    row = lax.broadcasted_iota(jnp.int32, (512, 1024), 0)
    la, lb = lane // 256, (lane // 64) % 4
    rank = jnp.where(even, la * 4 + lb, lb * 4 + la) * 32 + (lane // 16 % 4) * 8 + lane % 8
    spread = jnp.dot(
        basis[...], jnp.where(row == rank, 1.0, 0.0).astype(BF16), preferred_element_type=F32
    )
    lower = lax.broadcasted_iota(jnp.int32, (64, 1024), 1) // 8 % 2 == 0
    expand[0] = jnp.where(lower, spread, 0.0).astype(BF16)
    expand[1] = jnp.where(lower, 0.0, spread).astype(BF16)

    for copy in wait_z:
        copy.wait_recv()
    block = pl.ds(a * 16 + b * 4, 4)
    wait_b = [send(gathered.at[block], gathered.at[block], a_send.at[3 + k], a_recv.at[3 + k], b_peers[k]) for k in range(3)]
    for copy in wait_b:
        copy.wait_recv()
    block = pl.ds(a * 16, 16)
    wait_a = [send(gathered.at[block], gathered.at[block], a_send.at[6 + k], a_recv.at[6 + k], a_peers[k]) for k in range(3)]
    loads[1].wait()

    def project(total, a_):
        for b_ in range(4):
            at = pl.multiple_of(jnp.where(even, a_ * 4 + b_, b_ * 4 + a_) * 256, 256)
            rows = gathered[pl.ds(a_ * 16 + b_ * 4, 4)].reshape(256, 256)
            total += jnp.dot(grad[:, pl.ds(at, 256)], rows, preferred_element_type=F32)
        return total

    total = project(jnp.zeros((256, 256), F32), a)
    for k in (0, 2, 1):
        wait_a[k].wait_recv()
        total = project(total, (a + 3 - k) % 4)
    proj[core] = total.T.astype(BF16)
    half = send(proj.at[core], proj.at[core], p_send, p_recv, sibling)
    loads[2].wait()
    half.wait_recv()
    for load in loads[3:]:
        load.wait()

    waits = {}

    def stage_partial(c):
        first_column, _, padded = CHUNKS[c]
        for h in range(2):
            part = lax.dot_general(
                proj[h], hidden[pl.ds(first_column, padded)],
                (((1,), (1,)), ((), ())), preferred_element_type=F32,
            )
            for i in range(8):
                y_, x_ = (h * 8 + i) // 4, i % 4
                parts[c][jnp.where(even, y_ * 4 + x_, x_ * 4 + y_)] = part[i * 32 : i * 32 + 32].astype(BF16)
        waits["a", c] = [
            send(parts[c].at[pl.ds((a + k + 1) % 4 * 4, 4)], ras[c].at[k], c_send.at[c, k], c_recv.at[c, k], a_peers[k])
            for k in range(3)
        ]

    def stage_sum_a(c):
        for copy in waits["a", c]:
            copy.wait_recv()
        total = parts[c][pl.ds(a * 4, 4)].astype(F32)
        for k in range(3):
            total += ras[c][k].astype(F32)
        sas[c][...] = total.astype(BF16)
        waits["b", c] = [
            send(sas[c].at[(b + k + 1) % 4], rbs[c].at[k], c_send.at[c, 3 + k], c_recv.at[c, 3 + k], b_peers[k])
            for k in range(3)
        ]

    def stage_sum_b(c):
        padded = CHUNKS[c][2]
        total = parts[c][a * 4 + b].astype(F32)
        for k in range(3):
            total += ras[c][k, b].astype(F32)
        for copy in waits["b", c]:
            copy.wait_recv()
        for k in range(3):
            total += rbs[c][k].astype(F32)
        for z_ in range(4):
            block = pack(total[z_ * 8 : z_ * 8 + 8])
            szf[c, z_] = block
            sz[c, z_] = block.astype(BF16)
        waits["z", c] = [
            send(sz.at[c, (z + k + 1) % 4], rz.at[c, k], c_send.at[c, 6 + k], c_recv.at[c, 6 + k], z_peers[k])
            for k in range(3)
        ]

    def stage_moments(c):
        first_column, valid, _ = CHUNKS[c]
        at = pl.ds(first_column, valid)
        for copy in waits["z", c]:
            copy.wait_recv()
        total = szf[c, z]
        for k in range(3):
            total += rz[c, k].astype(F32)
        grad_low = unpack(total)[:, :valid]
        new_first = 0.9 * first[:, at] + 0.1 * grad_low
        new_second = 0.999 * second[:, at] + 0.001 * grad_low * grad_low
        new_first_ref[:, at] = new_first
        new_second_ref[:, at] = new_second
        dirs[:, at] = new_first / (jnp.sqrt(new_second) + 1e-08)
        steps[c, mine] = pack(dirs[:, pl.ds(first_column, 512)]).astype(BF16)
        waits["gz", c] = [
            send(steps.at[c, mine], steps.at[c, mine], c_send.at[c, 9 + k], c_recv.at[c, 9 + k], z_peers[k])
            for k in range(3)
        ]

    def stage_gather_b(c):
        for copy in waits["gz", c]:
            copy.wait_recv()
        block = pl.ds(a * 16 + b * 4, 4)
        waits["gb", c] = [
            send(steps.at[c, block], steps.at[c, block], c_send.at[c, 12 + k], c_recv.at[c, 12 + k], b_peers[k])
            for k in range(3)
        ]

    def stage_gather_a(c):
        for copy in waits["gb", c]:
            copy.wait_recv()
        block = pl.ds(a * 16, 16)
        waits["ga", c] = [
            send(steps.at[c, block], steps.at[c, block], c_send.at[c, 15 + k], c_recv.at[c, 15 + k], a_peers[k])
            for k in range(3)
        ]

    def slot(c, hi_, core_, rows=pl.ds(0, 64)):
        return slots_ref.at[hi_ * 2 + core_, rows, pl.ds(CHUNKS[c][0], CHUNKS[c][2])]

    top, bottom = pl.ds(0, 32), pl.ds(32, 32)
    own = []

    def stage_update(c):
        first_column, valid, padded = CHUNKS[c]
        for copy in waits["ga", c]:
            copy.wait_recv()
        every = steps[c].reshape(1024, HALF)
        update = jnp.concatenate(
            [jnp.dot(expand[h], every, preferred_element_type=F32) for h in range(2)], axis=1
        )[:, :valid]
        new = weight[:, pl.ds(first_column, valid)].astype(F32) - 0.1 * update
        local_new[:, pl.ds(first_column, valid)] = new.astype(BF16)
        src = local_new.at[:, pl.ds(first_column, padded)]
        waits["n", c] = send(src, slot(c, hi, core), c_send.at[c, 18], c_recv.at[c, 18], hi_next)
        waits["p", c] = send(src, slot(c, hi, core), c_send.at[c, 19], c_recv.at[c, 19], hi_prev)
        waits["s", c] = send(src, slot(c, hi, core), c_send.at[c, 20], c_recv.at[c, 20], sibling)
        copy = pltpu.make_async_copy(src, slot(c, hi, core), own_sem.at[c])
        copy.start()
        own.append(copy)

    def stage_forward(c):
        waits["n", c].wait_recv()
        prev = (hi + 3) % 4
        waits["n2", c] = send(slot(c, prev, core, top), slot(c, prev, core, top), c_send.at[c, 21], c_recv.at[c, 21], hi_next)
        waits["ns", c] = send(slot(c, prev, core), slot(c, prev, core), c_send.at[c, 22], c_recv.at[c, 22], sibling)
        waits["p", c].wait_recv()
        following = (hi + 1) % 4
        waits["p2", c] = send(slot(c, following, core, bottom), slot(c, following, core, bottom), c_send.at[c, 23], c_recv.at[c, 23], hi_prev)
        waits["ps", c] = send(slot(c, following, core), slot(c, following, core), c_send.at[c, 24], c_recv.at[c, 24], sibling)

    def stage_finish(c):
        far = (hi + 2) % 4
        waits["n2", c].wait_recv()
        waits["fs", c] = send(slot(c, far, core, top), slot(c, far, core, top), c_send.at[c, 25], c_recv.at[c, 25], sibling)
        waits["p2", c].wait_recv()
        waits["gs", c] = send(slot(c, far, core, bottom), slot(c, far, core, bottom), c_send.at[c, 26], c_recv.at[c, 26], sibling)

    stages = (
        stage_partial, stage_sum_a, stage_sum_b, stage_moments, stage_gather_b,
        stage_gather_a, stage_update, stage_forward, stage_finish,
    )
    n = len(CHUNKS)
    for step in range(len(stages) + n - 1):
        for c in range(n):
            if 0 <= step - c < len(stages):
                stages[step - c](c)
    for c in range(n):
        for name in ("s", "ns", "ps", "fs", "gs"):
            waits[name, c].wait_recv()
    for copy in own:
        copy.wait()
    for copy in sends:
        copy.wait_send()


def local(grad_out, hidden, proj_basis, weight, first_moment, second_moment):
    n = len(CHUNKS)
    wide = [padded for _, _, padded in CHUNKS]
    hbm = pl.BlockSpec(memory_space=pl.ANY)
    vmem = pl.BlockSpec(memory_space=pltpu.VMEM)
    dma = pltpu.SemaphoreType.DMA
    slots, new_first, new_second = pl.pallas_call(
        kernel,
        name="step",
        out_shape=(
            jax.ShapeDtypeStruct((8, 64, SLOT), BF16),
            jax.ShapeDtypeStruct((8, WIDTH), F32),
            jax.ShapeDtypeStruct((8, WIDTH), F32),
        ),
        in_specs=[hbm] * 6,
        out_specs=(hbm, vmem, vmem),
        scratch_shapes=[
            pltpu.VMEM((256, 4096), BF16),
            pltpu.VMEM((SLOT, 256), BF16),
            pltpu.VMEM((64, 512), BF16),
            pltpu.VMEM((64, WIDTH), BF16),
            pltpu.VMEM((8, WIDTH), F32),
            pltpu.VMEM((8, WIDTH), F32),
            dma((6,)),
            pltpu.VMEM((64, 64, 256), BF16),
            pltpu.VMEM((2, 64, 1024), BF16),
            pltpu.VMEM((2, 256, 256), BF16),
            pltpu.VMEM((8, 1536), F32),
            *[pltpu.VMEM((16, 32, w), BF16) for w in wide],
            *[pltpu.VMEM((3, 4, 32, w), BF16) for w in wide],
            *[pltpu.VMEM((4, 32, w), BF16) for w in wide],
            *[pltpu.VMEM((3, 32, w), BF16) for w in wide],
            pltpu.VMEM((n, 4, 16, HALF), BF16),
            pltpu.VMEM((n, 4, 16, HALF), F32),
            pltpu.VMEM((n, 3, 16, HALF), BF16),
            pltpu.VMEM((n, 64, 16, HALF), BF16),
            pltpu.VMEM((64, SLOT), BF16),
            dma((n,)),
            dma((9,)), dma((9,)), dma, dma, dma((n, 27)), dma((n, 27)),
        ],
        compiler_params=pltpu.CompilerParams(
            collective_id=0, has_side_effects=True, vmem_limit_bytes=40 * 2**20
        ),
    )(grad_out, hidden.T, proj_basis, weight, first_moment, second_moment)
    new_weight = jnp.concatenate([slots[t, :, :WIDTH] for t in range(8)], axis=1)
    return (new_weight, new_first, new_second)


def solution(mesh):
    return jax.shard_map(
        local,
        mesh=mesh,
        in_specs=(
            P("dp", None),
            P("dp", "tensor"),
            P("dp", None),
            P("dp", "tensor"),
            P("dp", "tensor"),
            P("dp", "tensor"),
        ),
        out_specs=(P("dp", None), P("dp", "tensor"), P("dp", "tensor")),
        check_vma=False,
    )
```

time: 1530 us -> 130 us (0.08)
  waiting for transfers between devices: 1500 us -> 0 us
  Pallas kernels: 0 us -> 119 us
    all_gather x3 -> x0, waiting for transfers between devices: 773 us -> none  [the longest x1 347 us: local(): lax.all_gather(direction, 'dp', axis=0, tiled=True)]
    unnamed x5 -> x0, waiting for transfers between devices: 726 us -> none
    pallas_call x0 -> x1, Pallas kernels: none -> 119 us  [local(): pl.pallas_call(kernel, name='step', out_shape=(jax.ShapeDtypeStruct((8, 6...]
  transfers between devices with their start and end apart: 4 -> 0, of which waited for: 4 -> 0; matrix products, arithmetic and copies ran while one was open for 0% -> 0% of each run, Pallas kernels for 0% -> 0%
where the time goes in v1:
time: 130 us; the launch traced here: 129 us
  Pallas kernels  119 us (92%)
  local copies, waits for them, and re-layouts  9.59 us (7%)
    pallas_call x1, Pallas kernels, local(): pl.pallas_call(kernel, name='step', out_shape=(jax.ShapeDtypeStruct((8, 6...  119 us
    unnamed x14, local copies, waits for them, and re-layouts  7.26 us

profile of v1, /device:TPU:1, one launch (start us, length us, event | category | flops | bytes accessed | tf_op | source)
XLA Modules:
  0.0 129.5 jit_solution(4597187092105623365)
XLA Ops:
  0.6 0.0 copy-start
  0.6 1.6 %copy-done = bf16[256,4096]{1,0:T(8,128)(2,1)S(1)} copy-done((bf16[256,4096]{1,0:T(8,128)(2,1)S(1)}, bf16[256,4096]{1,0:T(8,128)(2,1)}, u32[]{:S(2)}) %copy-start) | copy-done | bytes 2097176
  2.2 0.0 copy-start.1
  2.2 1.1 copy-done.1
  3.3 0.0 copy-start.2
  3.3 0.9 copy-done.2
  4.3 0.0 copy-start.3
  4.3 0.8 copy-done.3
  5.1 0.0 copy-start.4
  5.1 0.8 copy-done.4
  5.9 0.0 copy-start.5
  5.9 0.8 copy-done.5
  6.7 119.2 %step.1 = (bf16[8,64,1408]{2,1,0:T(8,128)(2,1)S(1)}, f32[8,1376]{1,0:T(8,128)S(1)}, f32[8,1376]{1,0:T(8,128)S(1)}) custom-call(bf16[256,4096]{1,0:T(8,128)(2,1)S(1)} %copy-done, bf16[1376,256]{1,0:T(8,128)(2,1)S(1)} %bitcast.17, bf16[64,512]{1,0:T(8,128)(2,1)S(1)} %copy-done.3, bf16[64,1376]{1,0:T(8,128)(2,1)S(1)} %copy-done.2, f32[8,1376]{1,0:T(8,128)S(1)} %copy-done.4, ...), custom_call_target="tpu_custom_call" | custom-call | tf_op jit(solution)/shard_map/step/pallas_call | solution.py:286
  125.9 0.1 slice_bitcast_fusion
  126.0 2.2 %concatenate.3 = bf16[64,11008]{1,0:T(8,128)(2,1)} concatenate(bf16[64,1376]{1,0:T(8,128)(2,1)S(1)} %get-tuple-element.16, bf16[64,1376]{1,0:T(8,128)(2,1)S(1)} %get-tuple-element.15, bf16[64,1376]{1,0:T(8,128)(2,1)S(1)} %get-tuple-element.14, bf16[64,1376]{1,0:T(8,128)(2,1)S(1)} %get-tuple-element.13, bf16[64,1376]{1,0:T(8,128)(2,1)S(1)} %get-tuple-element.12, ...), dimensions={1} | concatenate | bytes 2818048 | tf_op jit(solution)/shard_map/concatenate | solution.py:324
  128.2 0.6 copy.11
  128.9 0.6 copy.12
Async XLA Ops:
  0.6 1.6 %copy-start = (bf16[256,4096]{1,0:T(8,128)(2,1)S(1)}, bf16[256,4096]{1,0:T(8,128)(2,1)}, u32[]{:S(2)}) copy-start(bf16[256,4096]{1,0:T(8,128)(2,1)} %grad_ref.1) | copy-start | bytes 6291460
  2.2 1.1 copy-start.1
  3.3 0.9 copy-start.2
  4.3 0.8 copy-start.3
  5.1 0.8 copy-start.4
  5.9 0.8 copy-start.5

commit v2 on v1

--- a/solution.py
+++ b/solution.py
@@ -15,6 +15,7 @@
 CHUNKS = ((0, 512, 512), (512, 512, 512), (1024, 352, 384))
 HALF = 256
 SLOT = 1408
+ORDER = "P0 P1 S0 P2 M0 S1 G0 M1 S2 U0 G1 M2 U1 F0 G2 U2 F1 E0 F2 E1 E2"
 
 
 def pack(rows):
@@ -35,11 +36,10 @@
     slots_ref, new_first_ref, new_second_ref,
     grad, hidden, basis, weight, first, second, load_sem,
     gathered, expand, proj, dirs,
-    part0, part1, part2, ra0, ra1, ra2, sa0, sa1, sa2, rb0, rb1, rb2,
-    sz, szf, rz, steps, local_new, own_sem,
+    part0, part1, part2, ra0, ra1, ra2, sz, rz, steps, local_new, own_sem,
     a_send, a_recv, p_send, p_recv, c_send, c_recv,
 ):
-    parts, ras, sas, rbs = (part0, part1, part2), (ra0, ra1, ra2), (sa0, sa1, sa2), (rb0, rb1, rb2)
+    parts, ras = (part0, part1, part2), (ra0, ra1, ra2)
     dp, tensor = lax.axis_index("dp"), lax.axis_index("tensor")
     y, x, z = dp // 16, (dp // 4) % 4, dp % 4
     hi, core = tensor // 2, tensor % 2
@@ -92,40 +92,52 @@
     gathered[mine] = basis[:, columns]
     pl.semaphore_wait(barrier, len(friends))
 
-    wait_z = [send(gathered.at[mine], gathered.at[mine], a_send.at[k], a_recv.at[k], z_peers[k]) for k in range(3)]
-
-    lane = lax.broadcasted_iota(jnp.int32, (512, 1024), 1)
-    row = lax.broadcasted_iota(jnp.int32, (512, 1024), 0)
+    near = (1, 3, 2)
+    arrivals = {}
+
+    def pass_on(kb, kz, axes):
+        at = gathered.at[a * 16 + (b + 4 - kb) % 4 * 4 + (z + 4 - kz) % 4]
+        for axis in axes:
+            for k in near:
+                if axis == "z":
+                    index, to, key = k - 1, z_peers[k - 1], (0, 0, k)
+                elif axis == "b":
+                    index, to, key = 3 + kz * 3 + k - 1, b_peers[k - 1], (0, k, kz)
+                else:
+                    index, to, key = 15 + (kb * 4 + kz) * 3 + k - 1, a_peers[k - 1], (k, kb, kz)
+                arrivals[key] = send(at, at, a_send.at[index], a_recv.at[index], to)
+
+    pass_on(0, 0, "zba")
+    for kz in near:
+        arrivals[0, 0, kz].wait_recv()
+        pass_on(0, kz, "ba")
+    for kz in (0,) + near:
+        for kb in near:
+            arrivals[0, kb, kz].wait_recv()
+            pass_on(kb, kz, "a")
+
+    lane = lax.broadcasted_iota(jnp.int32, (1, 1024), 1)
     la, lb = lane // 256, (lane // 64) % 4
     rank = jnp.where(even, la * 4 + lb, lb * 4 + la) * 32 + (lane // 16 % 4) * 8 + lane % 8
+    row = lax.broadcasted_iota(jnp.int32, (512, 1024), 0)
     spread = jnp.dot(
         basis[...], jnp.where(row == rank, 1.0, 0.0).astype(BF16), preferred_element_type=F32
     )
-    lower = lax.broadcasted_iota(jnp.int32, (64, 1024), 1) // 8 % 2 == 0
+    lower = lane // 8 % 2 == 0
     expand[0] = jnp.where(lower, spread, 0.0).astype(BF16)
     expand[1] = jnp.where(lower, 0.0, spread).astype(BF16)
-
-    for copy in wait_z:
-        copy.wait_recv()
-    block = pl.ds(a * 16 + b * 4, 4)
-    wait_b = [send(gathered.at[block], gathered.at[block], a_send.at[3 + k], a_recv.at[3 + k], b_peers[k]) for k in range(3)]
-    for copy in wait_b:
-        copy.wait_recv()
-    block = pl.ds(a * 16, 16)
-    wait_a = [send(gathered.at[block], gathered.at[block], a_send.at[6 + k], a_recv.at[6 + k], a_peers[k]) for k in range(3)]
     loads[1].wait()
 
-    def project(total, a_):
-        for b_ in range(4):
+    total = jnp.zeros((256, 256), F32)
+    for kb in (0,) + near:
+        for ka in (0,) + near:
+            if ka:
+                for kz in range(4):
+                    arrivals[ka, kb, kz].wait_recv()
+            a_, b_ = (a + 4 - ka) % 4, (b + 4 - kb) % 4
             at = pl.multiple_of(jnp.where(even, a_ * 4 + b_, b_ * 4 + a_) * 256, 256)
             rows = gathered[pl.ds(a_ * 16 + b_ * 4, 4)].reshape(256, 256)
             total += jnp.dot(grad[:, pl.ds(at, 256)], rows, preferred_element_type=F32)
-        return total
-
-    total = project(jnp.zeros((256, 256), F32), a)
-    for k in (0, 2, 1):
-        wait_a[k].wait_recv()
-        total = project(total, (a + 3 - k) % 4)
     proj[core] = total.T.astype(BF16)
     half = send(proj.at[core], proj.at[core], p_send, p_recv, sibling)
     loads[2].wait()
@@ -156,37 +168,22 @@
         total = parts[c][pl.ds(a * 4, 4)].astype(F32)
         for k in range(3):
             total += ras[c][k].astype(F32)
-        sas[c][...] = total.astype(BF16)
-        waits["b", c] = [
-            send(sas[c].at[(b + k + 1) % 4], rbs[c].at[k], c_send.at[c, 3 + k], c_recv.at[c, 3 + k], b_peers[k])
-            for k in range(3)
-        ]
-
-    def stage_sum_b(c):
-        padded = CHUNKS[c][2]
-        total = parts[c][a * 4 + b].astype(F32)
-        for k in range(3):
-            total += ras[c][k, b].astype(F32)
-        for copy in waits["b", c]:
-            copy.wait_recv()
-        for k in range(3):
-            total += rbs[c][k].astype(F32)
-        for z_ in range(4):
-            block = pack(total[z_ * 8 : z_ * 8 + 8])
-            szf[c, z_] = block
-            sz[c, z_] = block.astype(BF16)
-        waits["z", c] = [
-            send(sz.at[c, (z + k + 1) % 4], rz.at[c, k], c_send.at[c, 6 + k], c_recv.at[c, 6 + k], z_peers[k])
-            for k in range(3)
+        for b_ in range(4):
+            for z_ in range(4):
+                sz[c, b_ * 4 + z_] = pack(total[b_, z_ * 8 : z_ * 8 + 8]).astype(BF16)
+        waits["bz", c] = [
+            send(sz.at[c, (b + kb) % 4 * 4 + (z + kz) % 4], rz.at[c, kb * 4 + kz],
+                 c_send.at[c, 2 + kb * 4 + kz], c_recv.at[c, 2 + kb * 4 + kz], device(a, (b + kb) % 4, (z + kz) % 4, hi, core))
+            for kb in range(4) for kz in range(4) if kb or kz
         ]
 
     def stage_moments(c):
         first_column, valid, _ = CHUNKS[c]
         at = pl.ds(first_column, valid)
-        for copy in waits["z", c]:
+        total = sz[c, b * 4 + z].astype(F32)
+        for copy in waits["bz", c]:
             copy.wait_recv()
-        total = szf[c, z]
-        for k in range(3):
+        for k in range(1, 16):
             total += rz[c, k].astype(F32)
         grad_low = unpack(total)[:, :valid]
         new_first = 0.9 * first[:, at] + 0.1 * grad_low
@@ -196,26 +193,17 @@
         dirs[:, at] = new_first / (jnp.sqrt(new_second) + 1e-08)
         steps[c, mine] = pack(dirs[:, pl.ds(first_column, 512)]).astype(BF16)
         waits["gz", c] = [
-            send(steps.at[c, mine], steps.at[c, mine], c_send.at[c, 9 + k], c_recv.at[c, 9 + k], z_peers[k])
+            send(steps.at[c, mine], steps.at[c, mine], c_send.at[c, 18 + k], c_recv.at[c, 18 + k], z_peers[k])
             for k in range(3)
         ]
 
-    def stage_gather_b(c):
+    def stage_gather(c):
         for copy in waits["gz", c]:
             copy.wait_recv()
-        block = pl.ds(a * 16 + b * 4, 4)
-        waits["gb", c] = [
-            send(steps.at[c, block], steps.at[c, block], c_send.at[c, 12 + k], c_recv.at[c, 12 + k], b_peers[k])
-            for k in range(3)
-        ]
-
-    def stage_gather_a(c):
-        for copy in waits["gb", c]:
-            copy.wait_recv()
-        block = pl.ds(a * 16, 16)
+        block = steps.at[c, pl.ds(a * 16 + b * 4, 4)]
         waits["ga", c] = [
-            send(steps.at[c, block], steps.at[c, block], c_send.at[c, 15 + k], c_recv.at[c, 15 + k], a_peers[k])
-            for k in range(3)
+            send(block, block, c_send.at[c, 20 + ka * 4 + kb], c_recv.at[c, 20 + ka * 4 + kb], device((a + ka) % 4, (b + kb) % 4, z, hi, core))
+            for ka in range(4) for kb in range(4) if ka or kb
         ]
 
     def slot(c, hi_, core_, rows=pl.ds(0, 64)):
@@ -235,9 +223,9 @@
         new = weight[:, pl.ds(first_column, valid)].astype(F32) - 0.1 * update
         local_new[:, pl.ds(first_column, valid)] = new.astype(BF16)
         src = local_new.at[:, pl.ds(first_column, padded)]
-        waits["n", c] = send(src, slot(c, hi, core), c_send.at[c, 18], c_recv.at[c, 18], hi_next)
-        waits["p", c] = send(src, slot(c, hi, core), c_send.at[c, 19], c_recv.at[c, 19], hi_prev)
-        waits["s", c] = send(src, slot(c, hi, core), c_send.at[c, 20], c_recv.at[c, 20], sibling)
+        waits["n", c] = send(src, slot(c, hi, core), c_send.at[c, 36], c_recv.at[c, 36], hi_next)
+        waits["p", c] = send(src, slot(c, hi, core), c_send.at[c, 37], c_recv.at[c, 37], hi_prev)
+        waits["s", c] = send(src, slot(c, hi, core), c_send.at[c, 38], c_recv.at[c, 38], sibling)
         copy = pltpu.make_async_copy(src, slot(c, hi, core), own_sem.at[c])
         copy.start()
         own.append(copy)
@@ -245,29 +233,26 @@
     def stage_forward(c):
         waits["n", c].wait_recv()
         prev = (hi + 3) % 4
-        waits["n2", c] = send(slot(c, prev, core, top), slot(c, prev, core, top), c_send.at[c, 21], c_recv.at[c, 21], hi_next)
-        waits["ns", c] = send(slot(c, prev, core), slot(c, prev, core), c_send.at[c, 22], c_recv.at[c, 22], sibling)
+        waits["n2", c] = send(slot(c, prev, core, top), slot(c, prev, core, top), c_send.at[c, 39], c_recv.at[c, 39], hi_next)
+        waits["ns", c] = send(slot(c, prev, core), slot(c, prev, core), c_send.at[c, 40], c_recv.at[c, 40], sibling)
         waits["p", c].wait_recv()
         following = (hi + 1) % 4
-        waits["p2", c] = send(slot(c, following, core, bottom), slot(c, following, core, bottom), c_send.at[c, 23], c_recv.at[c, 23], hi_prev)
-        waits["ps", c] = send(slot(c, following, core), slot(c, following, core), c_send.at[c, 24], c_recv.at[c, 24], sibling)
+        waits["p2", c] = send(slot(c, following, core, bottom), slot(c, following, core, bottom), c_send.at[c, 41], c_recv.at[c, 41], hi_prev)
+        waits["ps", c] = send(slot(c, following, core), slot(c, following, core), c_send.at[c, 42], c_recv.at[c, 42], sibling)
 
     def stage_finish(c):
         far = (hi + 2) % 4
         waits["n2", c].wait_recv()
-        waits["fs", c] = send(slot(c, far, core, top), slot(c, far, core, top), c_send.at[c, 25], c_recv.at[c, 25], sibling)
+        waits["fs", c] = send(slot(c, far, core, top), slot(c, far, core, top), c_send.at[c, 43], c_recv.at[c, 43], sibling)
         waits["p2", c].wait_recv()
-        waits["gs", c] = send(slot(c, far, core, bottom), slot(c, far, core, bottom), c_send.at[c, 26], c_recv.at[c, 26], sibling)
-
-    stages = (
-        stage_partial, stage_sum_a, stage_sum_b, stage_moments, stage_gather_b,
-        stage_gather_a, stage_update, stage_forward, stage_finish,
+        waits["gs", c] = send(slot(c, far, core, bottom), slot(c, far, core, bottom), c_send.at[c, 44], c_recv.at[c, 44], sibling)
+
+    stages = dict(
+        P=stage_partial, S=stage_sum_a, M=stage_moments, G=stage_gather, U=stage_update, F=stage_forward, E=stage_finish
     )
+    for item in ORDER.split():
+        stages[item[0]](int(item[1]))
     n = len(CHUNKS)
-    for step in range(len(stages) + n - 1):
-        for c in range(n):
-            if 0 <= step - c < len(stages):
-                stages[step - c](c)
     for c in range(n):
         for name in ("s", "ns", "ps", "fs", "gs"):
             waits[name, c].wait_recv()
@@ -307,18 +292,15 @@
             pltpu.VMEM((8, 1536), F32),
             *[pltpu.VMEM((16, 32, w), BF16) for w in wide],
             *[pltpu.VMEM((3, 4, 32, w), BF16) for w in wide],
-            *[pltpu.VMEM((4, 32, w), BF16) for w in wide],
-            *[pltpu.VMEM((3, 32, w), BF16) for w in wide],
-            pltpu.VMEM((n, 4, 16, HALF), BF16),
-            pltpu.VMEM((n, 4, 16, HALF), F32),
-            pltpu.VMEM((n, 3, 16, HALF), BF16),
+            pltpu.VMEM((n, 16, 16, HALF), BF16),
+            pltpu.VMEM((n, 16, 16, HALF), BF16),
             pltpu.VMEM((n, 64, 16, HALF), BF16),
             pltpu.VMEM((64, SLOT), BF16),
             dma((n,)),
-            dma((9,)), dma((9,)), dma, dma, dma((n, 27)), dma((n, 27)),
+            dma((63,)), dma((63,)), dma, dma, dma((n, 45)), dma((n, 45)),
         ],
         compiler_params=pltpu.CompilerParams(
-            collective_id=0, has_side_effects=True, vmem_limit_bytes=40 * 2**20
+            collective_id=0, has_side_effects=True, vmem_limit_bytes=62 * 2**20
         ),
     )(grad_out, hidden.T, proj_basis, weight, first_moment, second_moment)
     new_weight = jnp.concatenate([slots[t, :, :WIDTH] for t in range(8)], axis=1)

time: 130 us -> 102 us (0.78)
  Pallas kernels: 119 us -> 95.6 us
  local copies, waits for them, and re-layouts: 9.59 us -> 4.98 us
    pallas_call x1, Pallas kernels: 119 us -> 95.6 us  [local(): pl.pallas_call(kernel, name='step', out_shape=(jax.ShapeDtypeStruct((8, 6...]
    unnamed x14 -> x6, local copies, waits for them, and re-layouts: 7.26 us -> 1.25 us
    squeeze x1, local copies, waits for them, and re-layouts: 0.11 us -> 1.52 us  [local(): slots[t, :, :WIDTH]]
where the time goes in v2:
time: 102 us; the launch traced here: 101 us
  Pallas kernels  95.6 us (94%)
  local copies, waits for them, and re-layouts  4.98 us (5%)
    pallas_call x1, Pallas kernels, local(): pl.pallas_call(kernel, name='step', out_shape=(jax.ShapeDtypeStruct((8, 6...  95.6 us
    concatenate x1, local copies, waits for them, and re-layouts, local(): jnp.concatenate([slots[t, :, :WIDTH] for t in range(8)], axis=1)  2.21 us

profile of v2, /device:TPU:1, one launch (start us, length us, event | category | flops | bytes accessed | tf_op | source)
XLA Modules:
  0.0 101.2 jit_solution(16703671759771404591)
XLA Ops:
  0.6 95.6 %step.1 = (bf16[8,64,1408]{2,1,0:T(8,128)(2,1)}, f32[8,1376]{1,0:T(8,128)}, f32[8,1376]{1,0:T(8,128)}) custom-call(bf16[256,4096]{1,0:T(8,128)(2,1)} %grad_ref.1, bf16[1376,256]{1,0:T(8,128)(2,1)} %bitcast.17, bf16[64,512]{1,0:T(8,128)(2,1)} %basis_ref.1, bf16[64,1376]{1,0:T(8,128)(2,1)} %weight_ref.1, f32[8,1376]{1,0:T(8,128)} %first_ref.1, ...), custom_call_target="tpu_custom_call" | custom-call | tf_op jit(solution)/shard_map/step/pallas_call | solution.py:271
  96.2 1.5 %slice_bitcast_fusion = (bf16[64,1376]{1,0:T(8,128)(2,1)S(1)}, bf16[64,1376]{1,0:T(8,128)(2,1)S(1)}, bf16[64,1376]{1,0:T(8,128)(2,1)S(1)}, bf16[64,1376]{1,0:T(8...) fusion(bf16[8,64,1408]{2,1,0:T(8,128)(2,1)} %get-tuple-element.6), kind=kLoop, calls=%fused_computation | loop fusion | bytes 2818048 | tf_op jit(solution)/shard_map/squeeze | solution.py:306
  97.7 0.0 copy-start.1
  97.7 0.0 copy-start
  97.7 2.2 %concatenate.3 = bf16[64,11008]{1,0:T(8,128)(2,1)} concatenate(bf16[64,1376]{1,0:T(8,128)(2,1)S(1)} %get-tuple-element.16, bf16[64,1376]{1,0:T(8,128)(2,1)S(1)} %get-tuple-element.15, bf16[64,1376]{1,0:T(8,128)(2,1)S(1)} %get-tuple-element.14, bf16[64,1376]{1,0:T(8,128)(2,1)S(1)} %get-tuple-element.13, bf16[64,1376]{1,0:T(8,128)(2,1)S(1)} %get-tuple-element.12, ...), dimensions={1} | concatenate | bytes 2818048 | tf_op jit(solution)/shard_map/concatenate | solution.py:306
  99.9 0.0 copy-done.1
  99.9 0.6 copy.11
  100.6 0.0 copy-done
  100.6 0.6 copy.12
Async XLA Ops:
  97.7 2.2 %copy-start.1 = (f32[8,1376]{1,0:T(8,128)S(1)}, f32[8,1376]{1,0:T(8,128)}, u32[]{:S(2)}) copy-start(f32[8,1376]{1,0:T(8,128)} %get-tuple-element.21) | copy-start | bytes 132100
  97.7 2.8 %copy-start = (f32[8,1376]{1,0:T(8,128)S(1)}, f32[8,1376]{1,0:T(8,128)}, u32[]{:S(2)}) copy-start(f32[8,1376]{1,0:T(8,128)} %get-tuple-element.22) | copy-start | bytes 132100

commit v3 on v2

--- a/solution.py
+++ b/solution.py
@@ -15,7 +15,11 @@
 CHUNKS = ((0, 512, 512), (512, 512, 512), (1024, 352, 384))
 HALF = 256
 SLOT = 1408
-ORDER = "P0 P1 S0 P2 M0 S1 G0 M1 S2 U0 G1 M2 U1 F0 G2 U2 F1 E0 F2 E1 E2"
+ORDER = (
+    "C", "P0", "P1", "P2", "D", "C", "S0", "S1", "S2", "D", "C", "M0", "M1", "M2", "D", "C", "G0",
+    "G1", "G2", "D", "C", "H0", "H1", "H2", "U0", "D", "C", "U1", "U2", "D", "C", "F0", "F1", "D",
+    "C", "F2", "E0", "E1", "D", "E2",
+)
 
 
 def pack(rows):
@@ -92,7 +96,7 @@
     gathered[mine] = basis[:, columns]
     pl.semaphore_wait(barrier, len(friends))
 
-    near = (1, 3, 2)
+    near = (2, 1, 3)
     arrivals = {}
 
     def pass_on(kb, kz, axes):
@@ -159,7 +163,7 @@
                 parts[c][jnp.where(even, y_ * 4 + x_, x_ * 4 + y_)] = part[i * 32 : i * 32 + 32].astype(BF16)
         waits["a", c] = [
             send(parts[c].at[pl.ds((a + k + 1) % 4 * 4, 4)], ras[c].at[k], c_send.at[c, k], c_recv.at[c, k], a_peers[k])
-            for k in range(3)
+            for k in (1, 0, 2)
         ]
 
     def stage_sum_a(c):
@@ -174,7 +178,7 @@
         waits["bz", c] = [
             send(sz.at[c, (b + kb) % 4 * 4 + (z + kz) % 4], rz.at[c, kb * 4 + kz],
                  c_send.at[c, 2 + kb * 4 + kz], c_recv.at[c, 2 + kb * 4 + kz], device(a, (b + kb) % 4, (z + kz) % 4, hi, core))
-            for kb in range(4) for kz in range(4) if kb or kz
+            for kb in (2, 1, 3, 0) for kz in (3, 2, 1, 0) if kb or kz
         ]
 
     def stage_moments(c):
@@ -197,14 +201,26 @@
             for k in range(3)
         ]
 
+    def spread_a(c, kb):
+        block = steps.at[c, pl.ds(a * 16 + (b + 4 - kb) % 4 * 4, 4)]
+        waits["ga", c] += [
+            send(block, block, c_send.at[c, 23 + kb * 3 + k], c_recv.at[c, 23 + kb * 3 + k], a_peers[k - 1]) for k in near
+        ]
+
     def stage_gather(c):
         for copy in waits["gz", c]:
             copy.wait_recv()
         block = steps.at[c, pl.ds(a * 16 + b * 4, 4)]
-        waits["ga", c] = [
-            send(block, block, c_send.at[c, 20 + ka * 4 + kb], c_recv.at[c, 20 + ka * 4 + kb], device((a + ka) % 4, (b + kb) % 4, z, hi, core))
-            for ka in range(4) for kb in range(4) if ka or kb
-        ]
+        waits["gb", c] = {
+            k: send(block, block, c_send.at[c, 20 + k], c_recv.at[c, 20 + k], b_peers[k - 1]) for k in near
+        }
+        waits["ga", c] = []
+        spread_a(c, 0)
+
+    def stage_hand_on(c):
+        for kb in near:
+            waits["gb", c][kb].wait_recv()
+            spread_a(c, kb)
 
     def slot(c, hi_, core_, rows=pl.ds(0, 64)):
         return slots_ref.at[hi_ * 2 + core_, rows, pl.ds(CHUNKS[c][0], CHUNKS[c][2])]
@@ -248,18 +264,33 @@
         waits["gs", c] = send(slot(c, far, core, bottom), slot(c, far, core, bottom), c_send.at[c, 44], c_recv.at[c, 44], sibling)
 
     stages = dict(
-        P=stage_partial, S=stage_sum_a, M=stage_moments, G=stage_gather, U=stage_update, F=stage_forward, E=stage_finish
+        P=stage_partial, S=stage_sum_a, M=stage_moments, G=stage_gather, H=stage_hand_on, U=stage_update, F=stage_forward, E=stage_finish
     )
-    for item in ORDER.split():
-        stages[item[0]](int(item[1]))
+    drained = 0
+    for item in ORDER:
+        if item == "D":
+            for copy in sends[drained:checked]:
+                copy.wait_send()
+            drained = checked
+        elif item == "C":
+            checked = len(sends)
+        else:
+            stages[item[0]](int(item[1]))
     n = len(CHUNKS)
     for c in range(n):
         for name in ("s", "ns", "ps", "fs", "gs"):
             waits[name, c].wait_recv()
     for copy in own:
         copy.wait()
-    for copy in sends:
+    for copy in sends[drained:]:
         copy.wait_send()
+
+
+def assemble(slots_ref, first_ref, second_ref, weight_ref, new_first_ref, new_second_ref):
+    for t in range(8):
+        weight_ref[:, WIDTH * t : WIDTH * (t + 1)] = slots_ref[t, :, :WIDTH]
+    new_first_ref[...] = first_ref[...]
+    new_second_ref[...] = second_ref[...]
 
 
 def local(grad_out, hidden, proj_basis, weight, first_moment, second_moment):
@@ -303,8 +334,20 @@
             collective_id=0, has_side_effects=True, vmem_limit_bytes=62 * 2**20
         ),
     )(grad_out, hidden.T, proj_basis, weight, first_moment, second_moment)
-    new_weight = jnp.concatenate([slots[t, :, :WIDTH] for t in range(8)], axis=1)
-    return (new_weight, new_first, new_second)
+    moments = pl.BlockSpec((8, WIDTH), lambda i: (0, 0))
+    return pl.pallas_call(
+        assemble,
+        name="assemble",
+        grid=(2,),
+        out_shape=(
+            jax.ShapeDtypeStruct((64, 8 * WIDTH), BF16),
+            jax.ShapeDtypeStruct((8, WIDTH), F32),
+            jax.ShapeDtypeStruct((8, WIDTH), F32),
+        ),
+        in_specs=[pl.BlockSpec((8, 32, SLOT), lambda i: (0, i, 0)), moments, moments],
+        out_specs=(pl.BlockSpec((32, 8 * WIDTH), lambda i: (i, 0)), moments, moments),
+        compiler_params=pltpu.CompilerParams(vmem_limit_bytes=62 * 2**20),
+    )(slots, new_first, new_second)
 
 
 def solution(mesh):

time: 102 us -> 98.4 us (0.965)
  local copies, waits for them, and re-layouts: 4.98 us -> 0 us
  Pallas kernels: 95.6 us -> 97.6 us
    pallas_call x0 -> x1, Pallas kernels: none -> 2.47 us  [local(): pl.pallas_call(assemble, name='assemble', grid=(2,), out_shape=(jax.Shape...]
    concatenate x1 -> x0, local copies, waits for them, and re-layouts: 2.21 us -> none  [local(): jnp.concatenate([slots[t, :, :WIDTH] for t in range(8)], axis=1)]
    squeeze x1 -> x0, local copies, waits for them, and re-layouts: 1.52 us -> none  [local(): slots[t, :, :WIDTH]]
    unnamed x6 -> x0, local copies, waits for them, and re-layouts: 1.25 us -> none
where the time goes in v3:
time: 98.4 us; the launch traced here: 98.2 us
  Pallas kernels  97.6 us (99%)
    pallas_call x1, Pallas kernels, local(): pl.pallas_call(kernel, name='step', out_shape=(jax.ShapeDtypeStruct((8, 6...  95.1 us
    pallas_call x1, Pallas kernels, local(): pl.pallas_call(assemble, name='assemble', grid=(2,), out_shape=(jax.Shape...  2.47 us

profile of v3, /device:TPU:1, one launch (start us, length us, event | category | flops | bytes accessed | tf_op | source)
XLA Modules:
  0.0 98.2 jit_solution(6110237141889097515)
XLA Ops:
  0.6 95.1 %step.1 = (bf16[8,64,1408]{2,1,0:T(8,128)(2,1)}, f32[8,1376]{1,0:T(8,128)}, f32[8,1376]{1,0:T(8,128)}) custom-call(bf16[256,4096]{1,0:T(8,128)(2,1)} %grad_ref.1, bf16[1376,256]{1,0:T(8,128)(2,1)} %bitcast.1, bf16[64,512]{1,0:T(8,128)(2,1)} %basis_ref.1, bf16[64,1376]{1,0:T(8,128)(2,1)} %weight_ref.1, f32[8,1376]{1,0:T(8,128)} %first_ref.1, f32[8,1376]{1,0:T(8,128)} %second_ref.1), custom_call_target="tpu_custom_call" | custom-call | tf_op jit(solution)/shard_map/step/pallas_call | solution.py:302
  95.8 2.5 %assemble.1 = (bf16[64,11008]{1,0:T(8,128)(2,1)}, f32[8,1376]{1,0:T(8,128)}, f32[8,1376]{1,0:T(8,128)}) custom-call(bf16[8,64,1408]{2,1,0:T(8,128)(2,1)} %get-tuple-element.6.slots_ref, f32[8,1376]{1,0:T(8,128)} %get-tuple-element.7.first_ref, f32[8,1376]{1,0:T(8,128)} %get-tuple-element.8.second_ref), custom_call_target="tpu_custom_call" | custom-call | tf_op jit(solution)/shard_map/assemble/pallas_call | solution.py:338
